TPU v7x, 512 devices: a whole 4x4x16 slice. The times are simulated.
512 devices in a mesh: wide: 32 (over x_lo, z), narrow: 16 (over y, x_hi, core).
Axes of the slice: x: 4 (x_hi: 2, x_lo: 2; x = x_hi * 2 + x_lo), y: 4, z: 16, core: 2. Of those that a mesh axis runs over, the one named last changes fastest.
Arguments:
- batch: float32 [512, 768], P('wide'), may hold values from -9 to 9
- targets: float32 [512, 512], P(('wide', 'narrow')), may hold values from -6 to 6
- centers: float32 [65536, 768], P(('wide', 'narrow')), may hold values from -9 to 9
- weights: float32 [65536, 512], P(('wide', 'narrow')), may hold values from -6 to 6
Outputs:
- residual: float32 [512, 512], P(('wide', 'narrow'))
- new_weights: float32 [65536, 512], P(('wide', 'narrow'))
All inputs are finite; a program needn't handle non-finite values.
Results may differ from a plain program's by a relative error of at most 0.0001.
Values sent between devices are 32-bit elements; how exact they have to be, the bound alone decides.
A program may use at most 64 MiB of HBM per device.

v0:
```python
import math

import jax
import jax.numpy as jnp
from jax import lax
from jax.sharding import Mesh
from jax.sharding import PartitionSpec as P

WIDE = ("wide_0", "wide_1")
WIDE_NARROW = ("wide_0", "wide_1", "narrow")


def laid_out(tiles, dim):
    tiles = jnp.moveaxis(tiles, 0, dim)
    dims = tiles.shape
    return tiles.reshape(*dims[:dim], dims[dim] * dims[dim + 1], *dims[dim + 2 :])


def all_blocks(array, axes, order):
    tiles = array[None]
    for k in order:
        tiles = lax.all_gather(tiles, axes[k], axis=0, tiled=True)
    current = [lax.axis_size(axes[k]) for k in reversed(order)]
    tiles = tiles.reshape(*current, *array.shape)
    turned = sorted(range(len(order)), key=lambda place: order[len(order) - 1 - place])
    return tiles.transpose(*turned, *range(len(order), tiles.ndim)).reshape(-1, *array.shape)


def gather_axes(array, axes, order, dim):
    return laid_out(all_blocks(array, axes, order), dim)


def split_up(array, dim, devices):
    before, after = (array.shape[:dim], array.shape[dim + 1 :])
    return jnp.moveaxis(array.reshape(*before, devices, -1, *after), dim, 0)


def summed_on_arrival(array, axis, dim):
    tiles = split_up(array, dim, lax.axis_size(axis))
    arrived = lax.all_to_all(tiles, axis, split_axis=0, concat_axis=0, tiled=True)
    return arrived.sum(axis=0)


def sent_to_all(array, axis):
    devices = lax.axis_size(axis)
    return lax.all_to_all(
        jnp.broadcast_to(array[None], (devices, *array.shape)), axis, 0, 0, tiled=True
    )


def collect(array, axis, dim):
    return laid_out(sent_to_all(array, axis), dim)


def shards(batch, targets, centers, weights):
    local_count = centers.shape[0]
    features = centers.shape[1]
    center_total = local_count * lax.axis_size(WIDE) * lax.axis_size("narrow")
    pred_scale = 8.0 / math.sqrt(center_total)
    center_norms = jnp.sum(centers * centers, axis=1)
    piece = gather_axes(batch, WIDE, (0, 1), 0)
    row_norms = jnp.sum(piece * piece, axis=1)
    cross = jnp.dot(
        piece, centers.T, precision=lax.Precision.HIGHEST, preferred_element_type=jnp.float32
    )
    kernel = jnp.exp(-(row_norms[:, None] + center_norms[None, :] - 2.0 * cross) / features)
    all_rows = kernel.shape[0]
    partial_value = (
        jnp.dot(
            kernel, weights, precision=lax.Precision.HIGHEST, preferred_element_type=jnp.float32
        )
        * pred_scale
    )
    wide_sums = summed_on_arrival(partial_value, WIDE, 0)
    own_sums = summed_on_arrival(wide_sums, "narrow", 0)
    residual = own_sums - targets
    group_rows = collect(residual, "narrow", 0)
    residual_all = gather_axes(group_rows, WIDE, (0, 1), 0)
    change = lax.dot_general(
        kernel,
        residual_all,
        (((0,), (0,)), ((), ())),
        precision=lax.Precision.HIGHEST,
        preferred_element_type=jnp.float32,
    )
    new_weights = weights - 32.0 / all_rows * change
    return (residual, new_weights)


def solution(mesh):
    finer = Mesh(mesh.devices.reshape(2, 16, mesh.shape["narrow"]), ("wide_0", "wide_1", "narrow"))
    return jax.shard_map(
        shards,
        mesh=finer,
        in_specs=(P(WIDE, None), P(WIDE_NARROW, None), P(WIDE_NARROW, None), P(WIDE_NARROW, None)),
        out_specs=(P(WIDE_NARROW, None), P(WIDE_NARROW, None)),
        check_vma=False,
    )
```

profile of v0, /device:TPU:2, one launch (start us, length us, event | category | flops | bytes accessed | tf_op | source)
XLA Modules:
  0.0 247.5 jit_solution(9640493037348007649)
XLA Ops:
  7.2 0.0 all-gather.5.cloned.1.call-start
  7.2 10.4 %all-gather = f32[32,768]{1,0:T(8,128)} all-gather(f32[16,768]{1,0:T(8,128)} %param.4), channel_id=2, replica_groups=mesh['wide_0'=2,'wide_1'=16,'narrow'=16] {'wide_0'}, dimensions={0}, use_global_device_ids=true | all-gather | bytes 147456 | tf_op jit(solution)/shard_map/all_gather | solution.py:22
  17.6 0.0 all-gather.5.cloned.1.call-update
  17.6 0.0 all-gather.7.cloned.1.call-start
  17.6 1.1 multiply_reduce_fusion.1
  18.7 71.0 %all-gather.5.cloned.1.call-done = f32[32,16,768]{2,1,0:T(8,128)} async-done(((f32[2,16,768]{2,1,0:T(8,128)}), f32[32,16,768]{2,1,0:T(8,128)}) %all-gather.5.cloned.1.call-update) | async-done | bytes 1572880 | tf_op jit(solution)/shard_map/all_gather | solution.py:22
  89.7 0.0 copy-start
  89.7 1.6 copy.14
  91.4 0.2 copy-done
  91.6 0.0 copy-start.1
  91.6 0.0 copy-start.2
  91.6 0.2 multiply_reduce_fusion
  91.8 0.1 add.15
  91.9 0.7 copy-done.1
  92.6 1.4 fusion.3
  94.0 0.0 copy-done.2
  94.0 1.0 convolution_multiply_fusion
  95.0 0.0 copy-start.4
  95.0 50.6 %all_to_all.15 = f32[32,16,512]{2,1,0:T(8,128)S(1)} all-to-all(f32[32,16,512]{2,1,0:T(8,128)S(1)} %bitcast.23), channel_id=1, replica_groups=mesh['wide_0'=2,'wide_1'=16,'narrow'=16] {'wide_0','wide_1'}, dimensions={0} | all-to-all | bytes 2097152 | tf_op jit(solution)/shard_map/all_to_all | solution.py:40
  145.6 0.1 reduce_sum.40
  145.7 13.3 %all_to_all.16 = f32[16,1,512]{2,1,0:T(1,128)S(1)} all-to-all(f32[16,1,512]{2,1,0:T(1,128)S(1)} %reshape.26), channel_id=1, replica_groups=mesh['wide_0'=2,'wide_1'=16,'narrow'=16] {'narrow'}, dimensions={0} | all-to-all | bytes 65536 | tf_op jit(solution)/shard_map/all_to_all | solution.py:40
  159.1 0.0 copy-done.4
  159.1 0.0 copy-start.3
  159.1 10.1 %all_to_all.17 = f32[16,1,512]{2,1,0:T(1,128)S(1)} all-to-all(f32[16,1,512]{2,1,0:T(1,128)S(1)} %broadcast_in_dim.15), channel_id=1, replica_groups=mesh['wide_0'=2,'wide_1'=16,'narrow'=16] {'narrow'}, dimensions={0} | all-to-all | bytes 65536 | tf_op jit(solution)/shard_map/all_to_all | solution.py:46
  169.3 4.8 %all-gather.1 = f32[32,1,512]{2,1,0:T(1,128)S(1)} all-gather(f32[16,1,512]{2,1,0:T(1,128)S(1)} %all_to_all.17), channel_id=3, replica_groups=mesh['wide_0'=2,'wide_1'=16,'narrow'=16] {'wide_0'}, dimensions={0}, use_global_device_ids=true | all-gather | bytes 98304 | tf_op jit(solution)/shard_map/all_gather | solution.py:22
  174.0 0.6 copy.16
  174.7 0.0 all-gather.7.cloned.1.call-update
  174.7 63.1 %all-gather.7.cloned.1.call-done = f32[32,16,512]{2,1,0:T(8,128)} async-done(((f32[2,16,512]{2,1,0:T(8,128)}), f32[32,16,512]{2,1,0:T(8,128)}) %all-gather.7.cloned.1.call-update) | async-done | bytes 1048592 | tf_op jit(solution)/shard_map/all_gather | solution.py:22
  237.8 1.3 copy.15
  239.2 1.5 fusion.4
  240.6 0.0 copy-done.3
  (5 shorter events, 0.1 us)
Async XLA Ops:
  7.2 82.6 %all-gather.5.cloned.1.call-start = ((), (), s32[]{:S(2)}) async-start(), calls=%async_computation.3 | async-start | bytes 1671168 | tf_op jit(solution)/shard_map/all_gather | solution.py:22
  17.6 220.2 %all-gather.7.cloned.1.call-start = ((), (), s32[]{:S(2)}) async-start(), calls=%async_computation.4 | async-start | bytes 1114112 | tf_op jit(solution)/shard_map/all_gather | solution.py:22
  89.7 1.9 copy-start
  91.6 1.0 copy-start.1
  91.6 2.4 copy-start.2
  95.0 64.0 %copy-start.4 = (f32[1,512]{1,0:T(1,128)S(1)}, f32[1,512]{1,0:T(1,128)}, u32[]{:S(2)}) copy-start(f32[1,512]{1,0:T(1,128)} %param.5) | copy-start | bytes 6148
  159.1 81.6 %copy-start.3 = (f32[1,512]{1,0:T(1,128)}, f32[1,512]{1,0:T(1,128)S(1)}, u32[]{:S(2)}) copy-start(f32[1,512]{1,0:T(1,128)S(1)} %sub.10) | copy-start | bytes 6148
Sparse Core Ops, SparseCore 0:
  17.7 71.9 all-gather.4
  174.8 62.9 all-gather.6
where the time goes:
time: 248 us; the launch traced here: 247 us
  waiting for transfers between devices  134 us (54%)
  blocking collectives  89.2 us (36%)
  between operations  14.1 us (6%)
  local copies, waits for them, and re-layouts  4.68 us (2%)
  matrix products  3.85 us (2%)
    all_gather x2, waiting for transfers between devices, all_blocks(): tiles = lax.all_gather(tiles, axes[k], axis=0, tiled=True)  134 us
    all_to_all x2, blocking collectives, summed_on_arrival(): lax.all_to_all(tiles, axis, split_axis=0, concat_axis=0, tiled=True)  63.9 us
    all_gather x2, blocking collectives, all_blocks(): tiles = lax.all_gather(tiles, axes[k], axis=0, tiled=True)  15.2 us
    all_to_all x1, blocking collectives, sent_to_all(): lax.all_to_all(jnp.broadcast_to(array[None], (devices, *array.shape)), ax...  10.1 us
  transfers between devices with their start and end apart: 2, of which 2 were waited for; matrix products, arithmetic and copies ran while one was open for 0% of the time, Pallas kernels for 0%

commit v1 on v0

v1 whole, which is shorter than its diff:
```python
import functools
import math

import jax
import jax.numpy as jnp
from jax import lax
from jax.experimental import pallas as pl
from jax.experimental.pallas import tpu as pltpu
from jax.sharding import PartitionSpec as P

SIDE, DEPTH, CORES = 4, 16, 2
PLANE = SIDE * SIDE
GROUP = 8
NEAR = 4
MESH = pl.DeviceIdType.MESH
HI = lax.Precision.HIGHEST


def place():
    w, n = lax.axis_index("wide"), lax.axis_index("narrow")
    core, rest = lax.rem(n, CORES), lax.div(n, CORES)
    x_lo, z = lax.div(w, DEPTH), lax.rem(w, DEPTH)
    x_hi, y = lax.rem(rest, 2), lax.div(rest, 2)
    return x_hi * 2 + x_lo, y, z, core, n


def name_of(x, y, z, core):
    return (lax.rem(x, 2) * DEPTH + z, (y * 2 + lax.div(x, 2)) * CORES + core)


def body(
    pred_scale, step, batch_ref, targets_ref, centers_ref, weights_ref, res_ref, new_ref,
    xb, tg, cc, ww, z1, xa, cn, kk, pp, cb, s3, zb, rz, rb, uu, ub,
    lsem, core_s, core_r, az_s, az_r, ap_s, ap_r, cp_s, cp_r, cz_s, cz_r, dz_s, dz_r, dp_s, dp_r,
):
    x, y, z, core, n = place()
    features = cc.shape[2]
    m = cc.shape[1]
    lanes = 128
    xk = features // lanes
    rk = rb.shape[1] // lanes

    loads = [
        pltpu.make_async_copy(batch_ref, xb, lsem.at[0]),
        pltpu.make_async_copy(targets_ref, tg, lsem.at[1]),
        pltpu.make_async_copy(centers_ref, cc.at[0], lsem.at[2]),
        pltpu.make_async_copy(weights_ref, ww.at[0], lsem.at[3]),
    ]
    for load in loads:
        load.start()

    mate = name_of(x, y, z, 1 - core)
    z_peers = {d: name_of(x, y, lax.rem(z + d, DEPTH), core) for d in range(1, DEPTH)}
    p_peers = {
        q: name_of(lax.rem(x + q // SIDE, SIDE), lax.rem(y + q % SIDE, SIDE), z, core)
        for q in range(1, PLANE)
    }
    everyone = [mate, *z_peers.values(), *p_peers.values()]
    barrier = pltpu.get_barrier_semaphore()
    for peer in everyone:
        pl.semaphore_signal(barrier, inc=1, device_id=peer, device_id_type=MESH)

    def remote(src, dst, send, recv, peer):
        return pltpu.make_async_remote_copy(
            src_ref=src, dst_ref=dst, send_sem=send, recv_sem=recv,
            device_id=peer, device_id_type=MESH,
        )

    def opposite(q):
        return (-(q // SIDE)) % SIDE * SIDE + (-(q % SIDE)) % SIDE

    far_first = sorted(range(1, DEPTH), key=lambda d: -min(d, DEPTH - d))

    loads[0].wait()
    mine = xb[pl.ds(n, 1), :]
    for k in range(xk):
        z1[NEAR, k : k + 1, :] = mine[:, k * lanes : (k + 1) * lanes]
    loads[2].wait()
    loads[3].wait()
    loads[1].wait()
    pl.semaphore_wait(barrier, len(everyone))

    az = {
        d: remote(
            z1.at[NEAR], z1.at[(NEAR - d) % DEPTH], az_s.at[d], az_r.at[(NEAR - d) % DEPTH], z_peers[d]
        )
        for d in range(1, DEPTH)
    }
    for d in far_first:
        az[d].start()
    swap_c = remote(cc.at[0], cc.at[1], core_s.at[0], core_r.at[0], mate)
    swap_w = remote(ww.at[0], ww.at[1], core_s.at[1], core_r.at[1], mate)
    swap_c.start()
    swap_w.start()

    def landed_z(copies, s):
        copies[(NEAR - s) % DEPTH].wait_recv()

    ap = {}
    for g in range(2):
        rows = slice(g * GROUP, (g + 1) * GROUP)
        for s in range(g * GROUP, (g + 1) * GROUP):
            if s != NEAR:
                landed_z(az, s)
        for k in range(xk):
            xa[0, rows, k * lanes : (k + 1) * lanes] = z1[rows, k, :]
        for q in range(1, PLANE):
            ap[g, q] = remote(
                xa.at[0, pl.ds(g * GROUP, GROUP)],
                xa.at[opposite(q), pl.ds(g * GROUP, GROUP)],
                ap_s.at[g, q], ap_r.at[g, opposite(q)], p_peers[q],
            )
            ap[g, q].start()

    swap_c.wait_recv()
    both = cc[...].reshape(2 * m, features)
    ones = jnp.ones((8, features), jnp.float32)
    cn[...] = lax.dot_general(
        ones, both * both, (((1,), (1,)), ((), ())), precision=HI, preferred_element_type=jnp.float32
    )
    swap_w.wait_recv()

    cp = {}
    for g in range(2):
        rows = slice(g * GROUP, (g + 1) * GROUP)
        for q in range(1, PLANE):
            ap[g, opposite(q)].wait_recv()
        points = xa[:, rows, :].reshape(PLANE * GROUP, features)
        norms = jnp.sum(points * points, axis=1, keepdims=True)
        cross = lax.dot_general(
            points, cc[...].reshape(2 * m, features), (((1,), (1,)), ((), ())),
            precision=HI, preferred_element_type=jnp.float32,
        )
        kernel = jnp.exp(-(norms + cn[0:1, :] - 2.0 * cross) / features)
        kk[:, rows, :] = kernel.reshape(PLANE, GROUP, 2 * m)
        part = jnp.dot(
            kernel, ww[...].reshape(2 * m, -1), precision=HI, preferred_element_type=jnp.float32
        )
        pp[:, rows, :] = part.reshape(PLANE, GROUP, -1)
        for q in range(1, PLANE):
            cp[g, q] = remote(
                pp.at[q, pl.ds(g * GROUP, GROUP)],
                cb.at[opposite(q), pl.ds(g * GROUP, GROUP)],
                cp_s.at[g, q], cp_r.at[g, opposite(q)], p_peers[q],
            )
            cp[g, q].start()

    cz = {}
    for g in range(2):
        rows = slice(g * GROUP, (g + 1) * GROUP)
        for q in range(1, PLANE):
            cp[g, opposite(q)].wait_recv()
        total = pp[0, rows, :]
        for q in range(1, PLANE):
            total = total + cb[q, rows, :]
        for k in range(rk):
            s3[rows, k, :] = total[:, k * lanes : (k + 1) * lanes]
        for s in range(g * GROUP, (g + 1) * GROUP):
            d = (s - NEAR) % DEPTH
            if d:
                cz[d] = remote(
                    s3.at[s], zb.at[(NEAR - d) % DEPTH], cz_s.at[d], cz_r.at[(NEAR - d) % DEPTH], z_peers[d]
                )
                cz[d].start()

    own = s3[NEAR]
    for s in range(DEPTH):
        if s != NEAR:
            landed_z(cz, s)
            own = own + zb[s]
    own = own * pred_scale
    for k in range(rk):
        piece = own[k : k + 1, :] - tg[:, k * lanes : (k + 1) * lanes]
        rz[NEAR, k : k + 1, :] = piece
        res_ref[:, k * lanes : (k + 1) * lanes] = piece

    dz = {
        d: remote(
            rz.at[NEAR], rz.at[(NEAR - d) % DEPTH], dz_s.at[d], dz_r.at[(NEAR - d) % DEPTH], z_peers[d]
        )
        for d in range(1, DEPTH)
    }
    for d in far_first:
        dz[d].start()

    dp = {}
    for g in range(2):
        rows = slice(g * GROUP, (g + 1) * GROUP)
        for s in range(g * GROUP, (g + 1) * GROUP):
            if s != NEAR:
                landed_z(dz, s)
        for k in range(rk):
            rb[rows, k * lanes : (k + 1) * lanes] = rz[rows, k, :]
        for q in range(1, PLANE):
            here = pl.ds(g * GROUP, GROUP)
            there = pl.ds(opposite(q) * DEPTH + g * GROUP, GROUP)
            dp[g, q] = remote(
                rb.at[here], rb.at[there], dp_s.at[g, q], dp_r.at[g, opposite(q)], p_peers[q]
            )
            dp[g, q].start()

    for g in range(2):
        for q in range(1, PLANE):
            dp[g, opposite(q)].wait_recv()
    uu[...] = lax.dot_general(
        kk[...].reshape(PLANE * DEPTH, 2 * m), rb[...], (((0,), (0,)), ((), ())),
        precision=HI, preferred_element_type=jnp.float32,
    )
    swap_u = remote(uu.at[pl.ds(m, m)], ub, core_s.at[2], core_r.at[2], mate)
    swap_u.start()
    swap_u.wait_recv()
    new_ref[...] = ww[0] - step * (uu[0:m, :] + ub[...])

    swap_c.wait_send()
    swap_w.wait_send()
    swap_u.wait_send()
    for copies in (az, ap, cp, cz, dz, dp):
        for copy in copies.values():
            copy.wait_send()


def shards(batch, targets, centers, weights):
    m, features = centers.shape
    outputs = weights.shape[1]
    devices = lax.axis_size("wide") * lax.axis_size("narrow")
    all_rows = batch.shape[0] * lax.axis_size("wide")
    pred_scale = 8.0 / math.sqrt(m * devices)
    f32 = jnp.float32
    vmem = pltpu.VMEM
    dma = pltpu.SemaphoreType.DMA
    xk, rk = features // 128, outputs // 128
    rows = PLANE * DEPTH
    scratch = [
        vmem(batch.shape, f32),
        vmem(targets.shape, f32),
        vmem((2, m, features), f32),
        vmem((2, m, outputs), f32),
        vmem((DEPTH, xk, 128), f32),
        vmem((PLANE, DEPTH, features), f32),
        vmem((8, 2 * m), f32),
        vmem((PLANE, DEPTH, 2 * m), f32),
        vmem((PLANE, DEPTH, outputs), f32),
        vmem((PLANE, DEPTH, outputs), f32),
        vmem((DEPTH, rk, 128), f32),
        vmem((DEPTH, rk, 128), f32),
        vmem((DEPTH, rk, 128), f32),
        vmem((rows, outputs), f32),
        vmem((2 * m, outputs), f32),
        vmem((m, outputs), f32),
        dma((4,)),
        dma((3,)), dma((3,)),
        dma((DEPTH,)), dma((DEPTH,)),
        dma((2, PLANE)), dma((2, PLANE)),
        dma((2, PLANE)), dma((2, PLANE)),
        dma((DEPTH,)), dma((DEPTH,)),
        dma((DEPTH,)), dma((DEPTH,)),
        dma((2, PLANE)), dma((2, PLANE)),
    ]
    return pl.pallas_call(
        functools.partial(body, pred_scale, 32.0 / all_rows),
        out_shape=(
            jax.ShapeDtypeStruct(targets.shape, f32),
            jax.ShapeDtypeStruct(weights.shape, f32),
        ),
        in_specs=[pl.BlockSpec(memory_space=pl.ANY)] * 4,
        out_specs=(pl.BlockSpec(memory_space=pltpu.VMEM),) * 2,
        scratch_shapes=scratch,
        compiler_params=pltpu.CompilerParams(
            collective_id=0, has_side_effects=True, vmem_limit_bytes=50 << 20
        ),
    )(batch, targets, centers, weights)


def solution(mesh):
    both = P(("wide", "narrow"), None)
    return jax.shard_map(
        shards, mesh=mesh, in_specs=(P("wide", None), both, both, both), out_specs=(both, both), check_vma=False
    )
```

time: 248 us -> 73.7 us (0.30)
  the two profiles are of different devices: /device:TPU:2 before, /device:TPU:1 now
where the time goes in v1:
time: 73.7 us; the launch traced here: 73.5 us
  Pallas kernels  68.1 us (92%)
  local copies, waits for them, and re-layouts  4.7 us (6%)
    pallas_call x1, Pallas kernels, shards(): pl.pallas_call(functools.partial(body, pred_scale, 32.0 / all_rows), out_...  68.1 us
    unnamed x10, local copies, waits for them, and re-layouts  4.7 us

profile of v1, /device:TPU:1, one launch (start us, length us, event | category | flops | bytes accessed | tf_op | source)
XLA Modules:
  0.0 73.5 jit_solution(7605944837654651936)
XLA Ops:
  0.6 0.0 copy-start
  0.6 1.0 %copy-done = f32[128,768]{1,0:T(8,128)S(1)} copy-done((f32[128,768]{1,0:T(8,128)S(1)}, f32[128,768]{1,0:T(8,128)}, u32[]{:S(2)}) %copy-start) | copy-done | bytes 393240
  1.6 0.0 copy-start.1
  1.6 0.9 %copy-done.1 = f32[128,512]{1,0:T(8,128)S(1)} copy-done((f32[128,512]{1,0:T(8,128)S(1)}, f32[128,512]{1,0:T(8,128)}, u32[]{:S(2)}) %copy-start.1) | copy-done | bytes 262168
  2.6 0.0 copy-start.2
  2.6 0.8 %copy-done.2 = f32[16,768]{1,0:T(8,128)S(1)} copy-done((f32[16,768]{1,0:T(8,128)S(1)}, f32[16,768]{1,0:T(8,128)}, u32[]{:S(2)}) %copy-start.2) | copy-done | bytes 49176
  3.4 0.0 copy-start.3
  3.4 0.7 copy-done.3
  4.1 68.1 %shard_map.59 = (f32[1,512]{1,0:T(1,128)S(1)}, f32[128,512]{1,0:T(8,128)S(1)}) custom-call(f32[16,768]{1,0:T(8,128)S(1)} %copy-done.2, f32[1,512]{1,0:T(1,128)S(1)} %copy-done.3, f32[128,768]{1,0:T(8,128)S(1)} %copy-done, f32[128,512]{1,0:T(8,128)S(1)} %copy-done.1), custom_call_target="tpu_custom_call" | custom-call | tf_op jit(solution)/shard_map/pallas_call | solution.py:259
  72.2 0.6 copy.8
  72.8 0.7 copy.9
Async XLA Ops:
  0.6 1.0 %copy-start = (f32[128,768]{1,0:T(8,128)S(1)}, f32[128,768]{1,0:T(8,128)}, u32[]{:S(2)}) copy-start(f32[128,768]{1,0:T(8,128)} %centers_ref.1) | copy-start | bytes 1179652
  1.6 0.9 %copy-start.1 = (f32[128,512]{1,0:T(8,128)S(1)}, f32[128,512]{1,0:T(8,128)}, u32[]{:S(2)}) copy-start(f32[128,512]{1,0:T(8,128)} %weights_ref.1) | copy-start | bytes 786436
  2.6 0.8 %copy-start.2 = (f32[16,768]{1,0:T(8,128)S(1)}, f32[16,768]{1,0:T(8,128)}, u32[]{:S(2)}) copy-start(f32[16,768]{1,0:T(8,128)} %batch_ref.1) | copy-start | bytes 147460
  3.4 0.7 copy-start.3

commit v2 on v1

--- a/solution.py
+++ b/solution.py
@@ -11,6 +11,7 @@
 SIDE, DEPTH, CORES = 4, 16, 2
 PLANE = SIDE * SIDE
 GROUP = 8
+REACH = 4
 NEAR = 4
 MESH = pl.DeviceIdType.MESH
 HI = lax.Precision.HIGHEST
@@ -38,7 +39,7 @@
     m = cc.shape[1]
     lanes = 128
     xk = features // lanes
-    rk = rb.shape[1] // lanes
+    rk = rb.shape[2] // lanes
 
     loads = [
         pltpu.make_async_copy(batch_ref, xb, lsem.at[0]),
@@ -55,9 +56,10 @@
         q: name_of(lax.rem(x + q // SIDE, SIDE), lax.rem(y + q % SIDE, SIDE), z, core)
         for q in range(1, PLANE)
     }
-    everyone = [mate, *z_peers.values(), *p_peers.values()]
+    greeted = [mate, *p_peers.values()]
+    greeted += [z_peers[d % DEPTH] for d in range(-REACH, REACH + 1) if d]
     barrier = pltpu.get_barrier_semaphore()
-    for peer in everyone:
+    for peer in greeted:
         pl.semaphore_signal(barrier, inc=1, device_id=peer, device_id_type=MESH)
 
     def remote(src, dst, send, recv, peer):
@@ -66,6 +68,15 @@
             device_id=peer, device_id_type=MESH,
         )
 
+    sent = []
+
+    def go(copy):
+        copy.start()
+        sent.append(copy)
+
+    def arrive(copy):
+        copy.wait_recv()
+
     def opposite(q):
         return (-(q // SIDE)) % SIDE * SIDE + (-(q % SIDE)) % SIDE
 
@@ -75,33 +86,35 @@
     mine = xb[pl.ds(n, 1), :]
     for k in range(xk):
         z1[NEAR, k : k + 1, :] = mine[:, k * lanes : (k + 1) * lanes]
+    pl.semaphore_wait(barrier, len(greeted))
+
+    az = {}
+
+    def along_z(source, d, slot):
+        az[slot] = remote(z1.at[source], z1.at[slot], az_s.at[slot], az_r.at[slot], z_peers[d % DEPTH])
+        go(az[slot])
+
+    for d in (4, -4, 3, -3, 2, -2, 1, -1):
+        along_z(NEAR, d, NEAR - d)
     loads[2].wait()
+    swap_c = remote(cc.at[0], cc.at[1], core_s.at[0], core_r.at[0], mate)
+    go(swap_c)
     loads[3].wait()
-    loads[1].wait()
-    pl.semaphore_wait(barrier, len(everyone))
-
-    az = {
-        d: remote(
-            z1.at[NEAR], z1.at[(NEAR - d) % DEPTH], az_s.at[d], az_r.at[(NEAR - d) % DEPTH], z_peers[d]
-        )
-        for d in range(1, DEPTH)
-    }
-    for d in far_first:
-        az[d].start()
-    swap_c = remote(cc.at[0], cc.at[1], core_s.at[0], core_r.at[0], mate)
     swap_w = remote(ww.at[0], ww.at[1], core_s.at[1], core_r.at[1], mate)
-    swap_c.start()
-    swap_w.start()
-
-    def landed_z(copies, s):
-        copies[(NEAR - s) % DEPTH].wait_recv()
+    go(swap_w)
+    for s in (3, 5, 2, 6, 1, 7, 0):
+        arrive(az[s])
+        if s < NEAR:
+            along_z(s, REACH, s + 12)
+        else:
+            along_z(s, -REACH, s + 4)
 
     ap = {}
     for g in range(2):
         rows = slice(g * GROUP, (g + 1) * GROUP)
-        for s in range(g * GROUP, (g + 1) * GROUP):
-            if s != NEAR:
-                landed_z(az, s)
+        if g == 1:
+            for s in range(GROUP, DEPTH):
+                arrive(az[s])
         for k in range(xk):
             xa[0, rows, k * lanes : (k + 1) * lanes] = z1[rows, k, :]
         for q in range(1, PLANE):
@@ -110,21 +123,25 @@
                 xa.at[opposite(q), pl.ds(g * GROUP, GROUP)],
                 ap_s.at[g, q], ap_r.at[g, opposite(q)], p_peers[q],
             )
-            ap[g, q].start()
-
-    swap_c.wait_recv()
+            go(ap[g, q])
+
+    def landed_z(copies, s):
+        arrive(copies[(NEAR - s) % DEPTH])
+
+    loads[1].wait()
+    arrive(swap_c)
     both = cc[...].reshape(2 * m, features)
     ones = jnp.ones((8, features), jnp.float32)
     cn[...] = lax.dot_general(
         ones, both * both, (((1,), (1,)), ((), ())), precision=HI, preferred_element_type=jnp.float32
     )
-    swap_w.wait_recv()
+    arrive(swap_w)
 
     cp = {}
     for g in range(2):
         rows = slice(g * GROUP, (g + 1) * GROUP)
         for q in range(1, PLANE):
-            ap[g, opposite(q)].wait_recv()
+            arrive(ap[g, opposite(q)])
         points = xa[:, rows, :].reshape(PLANE * GROUP, features)
         norms = jnp.sum(points * points, axis=1, keepdims=True)
         cross = lax.dot_general(
@@ -143,13 +160,13 @@
                 cb.at[opposite(q), pl.ds(g * GROUP, GROUP)],
                 cp_s.at[g, q], cp_r.at[g, opposite(q)], p_peers[q],
             )
-            cp[g, q].start()
+            go(cp[g, q])
 
     cz = {}
     for g in range(2):
         rows = slice(g * GROUP, (g + 1) * GROUP)
         for q in range(1, PLANE):
-            cp[g, opposite(q)].wait_recv()
+            arrive(cp[g, opposite(q)])
         total = pp[0, rows, :]
         for q in range(1, PLANE):
             total = total + cb[q, rows, :]
@@ -161,7 +178,7 @@
                 cz[d] = remote(
                     s3.at[s], zb.at[(NEAR - d) % DEPTH], cz_s.at[d], cz_r.at[(NEAR - d) % DEPTH], z_peers[d]
                 )
-                cz[d].start()
+                go(cz[d])
 
     own = s3[NEAR]
     for s in range(DEPTH):
@@ -181,7 +198,7 @@
         for d in range(1, DEPTH)
     }
     for d in far_first:
-        dz[d].start()
+        go(dz[d])
 
     dp = {}
     for g in range(2):
@@ -190,33 +207,34 @@
             if s != NEAR:
                 landed_z(dz, s)
         for k in range(rk):
-            rb[rows, k * lanes : (k + 1) * lanes] = rz[rows, k, :]
-        for q in range(1, PLANE):
-            here = pl.ds(g * GROUP, GROUP)
-            there = pl.ds(opposite(q) * DEPTH + g * GROUP, GROUP)
+            rb[0, rows, k * lanes : (k + 1) * lanes] = rz[rows, k, :]
+        for q in range(1, PLANE):
             dp[g, q] = remote(
-                rb.at[here], rb.at[there], dp_s.at[g, q], dp_r.at[g, opposite(q)], p_peers[q]
+                rb.at[0, pl.ds(g * GROUP, GROUP)],
+                rb.at[opposite(q), pl.ds(g * GROUP, GROUP)],
+                dp_s.at[g, q], dp_r.at[g, opposite(q)], p_peers[q],
             )
-            dp[g, q].start()
-
-    for g in range(2):
-        for q in range(1, PLANE):
-            dp[g, opposite(q)].wait_recv()
-    uu[...] = lax.dot_general(
-        kk[...].reshape(PLANE * DEPTH, 2 * m), rb[...], (((0,), (0,)), ((), ())),
-        precision=HI, preferred_element_type=jnp.float32,
-    )
+            go(dp[g, q])
+
+    change = None
+    for g in range(2):
+        rows = slice(g * GROUP, (g + 1) * GROUP)
+        for q in range(1, PLANE):
+            arrive(dp[g, opposite(q)])
+        term = lax.dot_general(
+            kk[:, rows, :].reshape(PLANE * GROUP, 2 * m),
+            rb[:, rows, :].reshape(PLANE * GROUP, -1),
+            (((0,), (0,)), ((), ())), precision=HI, preferred_element_type=jnp.float32,
+        )
+        change = term if change is None else change + term
+    uu[...] = change
     swap_u = remote(uu.at[pl.ds(m, m)], ub, core_s.at[2], core_r.at[2], mate)
-    swap_u.start()
-    swap_u.wait_recv()
+    go(swap_u)
+    arrive(swap_u)
     new_ref[...] = ww[0] - step * (uu[0:m, :] + ub[...])
 
-    swap_c.wait_send()
-    swap_w.wait_send()
-    swap_u.wait_send()
-    for copies in (az, ap, cp, cz, dz, dp):
-        for copy in copies.values():
-            copy.wait_send()
+    for copy in sent:
+        copy.wait_send()
 
 
 def shards(batch, targets, centers, weights):
@@ -229,7 +247,6 @@
     vmem = pltpu.VMEM
     dma = pltpu.SemaphoreType.DMA
     xk, rk = features // 128, outputs // 128
-    rows = PLANE * DEPTH
     scratch = [
         vmem(batch.shape, f32),
         vmem(targets.shape, f32),
@@ -244,7 +261,7 @@
         vmem((DEPTH, rk, 128), f32),
         vmem((DEPTH, rk, 128), f32),
         vmem((DEPTH, rk, 128), f32),
-        vmem((rows, outputs), f32),
+        vmem((PLANE, DEPTH, outputs), f32),
         vmem((2 * m, outputs), f32),
         vmem((m, outputs), f32),
         dma((4,)),
@@ -262,11 +279,11 @@
             jax.ShapeDtypeStruct(targets.shape, f32),
             jax.ShapeDtypeStruct(weights.shape, f32),
         ),
-        in_specs=[pl.BlockSpec(memory_space=pl.ANY)] * 4,
+        in_specs=[pl.BlockSpec(memory_space=pltpu.HBM)] * 4,
         out_specs=(pl.BlockSpec(memory_space=pltpu.VMEM),) * 2,
         scratch_shapes=scratch,
         compiler_params=pltpu.CompilerParams(
-            collective_id=0, has_side_effects=True, vmem_limit_bytes=50 << 20
+            collective_id=0, has_side_effects=True, vmem_limit_bytes=(64 << 20) - (160 << 10)
         ),
     )(batch, targets, centers, weights)
 

time: 73.7 us -> 71 us (0.963)
  local copies, waits for them, and re-layouts: 4.7 us -> 2.92 us
  Pallas kernels: 68.1 us -> 67.2 us
    unnamed x10 -> x4, local copies, waits for them, and re-layouts: 4.7 us -> 2.92 us
    pallas_call x1, Pallas kernels: 68.1 us -> 67.2 us  [shards(): pl.pallas_call(functools.partial(body, pred_scale, 32.0 / all_rows), out_...]
where the time goes in v2:
time: 71 us; the launch traced here: 70.8 us
  Pallas kernels  67.2 us (95%)
  local copies, waits for them, and re-layouts  2.92 us (4%)
    pallas_call x1, Pallas kernels, shards(): pl.pallas_call(functools.partial(body, pred_scale, 32.0 / all_rows), out_...  67.2 us
    unnamed x4, local copies, waits for them, and re-layouts  2.92 us

profile of v2, /device:TPU:1, one launch (start us, length us, event | category | flops | bytes accessed | tf_op | source)
XLA Modules:
  0.0 70.8 jit_solution(15464499656887409534)
XLA Ops:
  0.6 67.2 %shard_map.59 = (f32[1,512]{1,0:T(1,128)}, f32[128,512]{1,0:T(8,128)}) custom-call(f32[16,768]{1,0:T(8,128)} %batch_ref.1, f32[1,512]{1,0:T(1,128)} %targets_ref.1, f32[128,768]{1,0:T(8,128)} %centers_ref.1, f32[128,512]{1,0:T(8,128)} %weights_ref.1), custom_call_target="tpu_custom_call" | custom-call | tf_op jit(solution)/shard_map/pallas_call | solution.py:276
  67.9 0.0 copy-start
  67.9 0.7 copy-done
  68.6 0.6 copy.8
  69.1 1.7 %copy.9 = f32[128,512]{1,0:T(8,128)} copy(f32[128,512]{1,0:T(8,128)} %get-tuple-element.5) | data formatting | bytes 524288
Async XLA Ops:
  67.9 0.7 copy-start

commit v3 on v2

--- a/solution.py
+++ b/solution.py
@@ -27,6 +27,10 @@
 
 def name_of(x, y, z, core):
     return (lax.rem(x, 2) * DEPTH + z, (y * 2 + lax.div(x, 2)) * CORES + core)
+
+
+def hops(d):
+    return min(d, SIDE - d)
 
 
 def body(
@@ -77,12 +81,16 @@
     def arrive(copy):
         copy.wait_recv()
 
+    def got(copy):
+        copy.wait()
+
     def opposite(q):
         return (-(q // SIDE)) % SIDE * SIDE + (-(q % SIDE)) % SIDE
 
     far_first = sorted(range(1, DEPTH), key=lambda d: -min(d, DEPTH - d))
-
-    loads[0].wait()
+    plane_far_first = sorted(range(1, PLANE), key=lambda q: -hops(q // SIDE) - hops(q % SIDE))
+
+    got(loads[0])
     mine = xb[pl.ds(n, 1), :]
     for k in range(xk):
         z1[NEAR, k : k + 1, :] = mine[:, k * lanes : (k + 1) * lanes]
@@ -96,10 +104,10 @@
 
     for d in (4, -4, 3, -3, 2, -2, 1, -1):
         along_z(NEAR, d, NEAR - d)
-    loads[2].wait()
+    got(loads[2])
     swap_c = remote(cc.at[0], cc.at[1], core_s.at[0], core_r.at[0], mate)
     go(swap_c)
-    loads[3].wait()
+    got(loads[3])
     swap_w = remote(ww.at[0], ww.at[1], core_s.at[1], core_r.at[1], mate)
     go(swap_w)
     for s in (3, 5, 2, 6, 1, 7, 0):
@@ -117,7 +125,7 @@
                 arrive(az[s])
         for k in range(xk):
             xa[0, rows, k * lanes : (k + 1) * lanes] = z1[rows, k, :]
-        for q in range(1, PLANE):
+        for q in plane_far_first:
             ap[g, q] = remote(
                 xa.at[0, pl.ds(g * GROUP, GROUP)],
                 xa.at[opposite(q), pl.ds(g * GROUP, GROUP)],
@@ -128,7 +136,7 @@
     def landed_z(copies, s):
         arrive(copies[(NEAR - s) % DEPTH])
 
-    loads[1].wait()
+    got(loads[1])
     arrive(swap_c)
     both = cc[...].reshape(2 * m, features)
     ones = jnp.ones((8, features), jnp.float32)
@@ -138,29 +146,35 @@
     arrive(swap_w)
 
     cp = {}
-    for g in range(2):
-        rows = slice(g * GROUP, (g + 1) * GROUP)
-        for q in range(1, PLANE):
-            arrive(ap[g, opposite(q)])
-        points = xa[:, rows, :].reshape(PLANE * GROUP, features)
-        norms = jnp.sum(points * points, axis=1, keepdims=True)
-        cross = lax.dot_general(
-            points, cc[...].reshape(2 * m, features), (((1,), (1,)), ((), ())),
-            precision=HI, preferred_element_type=jnp.float32,
-        )
-        kernel = jnp.exp(-(norms + cn[0:1, :] - 2.0 * cross) / features)
-        kk[:, rows, :] = kernel.reshape(PLANE, GROUP, 2 * m)
-        part = jnp.dot(
-            kernel, ww[...].reshape(2 * m, -1), precision=HI, preferred_element_type=jnp.float32
-        )
-        pp[:, rows, :] = part.reshape(PLANE, GROUP, -1)
-        for q in range(1, PLANE):
+
+    def send_parts(g):
+        for q in plane_far_first:
             cp[g, q] = remote(
                 pp.at[q, pl.ds(g * GROUP, GROUP)],
                 cb.at[opposite(q), pl.ds(g * GROUP, GROUP)],
                 cp_s.at[g, q], cp_r.at[g, opposite(q)], p_peers[q],
             )
             go(cp[g, q])
+
+    for g in range(2):
+        rows = slice(g * GROUP, (g + 1) * GROUP)
+        for q in range(1, PLANE):
+            arrive(ap[g, opposite(q)])
+        if g == 1:
+            send_parts(0)
+        points = xa[:, rows, :].reshape(PLANE * GROUP, features)
+        norms = jnp.sum(points * points, axis=1, keepdims=True)
+        cross = lax.dot_general(
+            points, cc[...].reshape(2 * m, features), (((1,), (1,)), ((), ())),
+            precision=HI, preferred_element_type=jnp.float32,
+        )
+        kernel = jnp.exp(-(norms + cn[0:1, :] - 2.0 * cross) / features)
+        kk[:, rows, :] = kernel.reshape(PLANE, GROUP, 2 * m)
+        part = jnp.dot(
+            kernel, ww[...].reshape(2 * m, -1), precision=HI, preferred_element_type=jnp.float32
+        )
+        pp[:, rows, :] = part.reshape(PLANE, GROUP, -1)
+    send_parts(1)
 
     cz = {}
     for g in range(2):
@@ -172,9 +186,9 @@
             total = total + cb[q, rows, :]
         for k in range(rk):
             s3[rows, k, :] = total[:, k * lanes : (k + 1) * lanes]
-        for s in range(g * GROUP, (g + 1) * GROUP):
-            d = (s - NEAR) % DEPTH
-            if d:
+        for d in far_first:
+            s = (NEAR + d) % DEPTH
+            if s // GROUP == g:
                 cz[d] = remote(
                     s3.at[s], zb.at[(NEAR - d) % DEPTH], cz_s.at[d], cz_r.at[(NEAR - d) % DEPTH], z_peers[d]
                 )
@@ -208,7 +222,7 @@
                 landed_z(dz, s)
         for k in range(rk):
             rb[0, rows, k * lanes : (k + 1) * lanes] = rz[rows, k, :]
-        for q in range(1, PLANE):
+        for q in plane_far_first:
             dp[g, q] = remote(
                 rb.at[0, pl.ds(g * GROUP, GROUP)],
                 rb.at[opposite(q), pl.ds(g * GROUP, GROUP)],

time: 71 us -> 67.9 us (0.956)
  Pallas kernels: 67.2 us -> 64.1 us
    pallas_call x1, Pallas kernels: 67.2 us -> 64.1 us  [shards(): pl.pallas_call(functools.partial(body, pred_scale, 32.0 / all_rows), out_...]
where the time goes in v3:
time: 67.9 us; the launch traced here: 67.7 us
  Pallas kernels  64.1 us (94%)
  local copies, waits for them, and re-layouts  2.92 us (4%)
    pallas_call x1, Pallas kernels, shards(): pl.pallas_call(functools.partial(body, pred_scale, 32.0 / all_rows), out_...  64.1 us
    unnamed x4, local copies, waits for them, and re-layouts  2.92 us

profile of v3, /device:TPU:1, one launch (start us, length us, event | category | flops | bytes accessed | tf_op | source)
XLA Modules:
  0.0 67.7 jit_solution(14026210512234096923)
XLA Ops:
  0.6 64.1 %shard_map.59 = (f32[1,512]{1,0:T(1,128)}, f32[128,512]{1,0:T(8,128)}) custom-call(f32[16,768]{1,0:T(8,128)} %batch_ref.1, f32[1,512]{1,0:T(1,128)} %targets_ref.1, f32[128,768]{1,0:T(8,128)} %centers_ref.1, f32[128,512]{1,0:T(8,128)} %weights_ref.1), custom_call_target="tpu_custom_call" | custom-call | tf_op jit(solution)/shard_map/pallas_call | solution.py:290
  64.8 0.0 copy-start
  64.8 0.7 copy-done
  65.5 0.6 copy.8
  66.0 1.7 %copy.9 = f32[128,512]{1,0:T(8,128)} copy(f32[128,512]{1,0:T(8,128)} %get-tuple-element.5) | data formatting | bytes 524288
Async XLA Ops:
  64.8 0.7 %copy-start = (f32[1,512]{1,0:T(1,128)S(1)}, f32[1,512]{1,0:T(1,128)}, u32[]{:S(2)}) copy-start(f32[1,512]{1,0:T(1,128)} %get-tuple-element.4) | copy-start | bytes 6148

commit v4 on v3

--- a/solution.py
+++ b/solution.py
@@ -29,13 +29,28 @@
     return (lax.rem(x, 2) * DEPTH + z, (y * 2 + lax.div(x, 2)) * CORES + core)
 
 
+def halves(v):
+    top = v.astype(jnp.bfloat16)
+    return top, (v - top.astype(jnp.float32)).astype(jnp.bfloat16)
+
+
+def product(a, b, dims, last):
+    def dot(u, v):
+        return lax.dot_general(u, v, (dims, ((), ())), preferred_element_type=jnp.float32)
+
+    low = dot(a[0], b[1]) + dot(a[1], b[0])
+    if last:
+        low = low + dot(a[1], b[1])
+    return dot(a[0], b[0]) + low
+
+
 def hops(d):
     return min(d, SIDE - d)
 
 
 def body(
     pred_scale, step, batch_ref, targets_ref, centers_ref, weights_ref, res_ref, new_ref,
-    xb, tg, cc, ww, z1, xa, cn, kk, pp, cb, s3, zb, rz, rb, uu, ub,
+    xb, tg, cc, ww, ch, wh, z1, xa, cn, kt, pp, cb, s3, zb, rz, rb, uu, ub,
     lsem, core_s, core_r, az_s, az_r, ap_s, ap_r, cp_s, cp_r, cz_s, cz_r, dz_s, dz_r, dp_s, dp_r,
 ):
     x, y, z, core, n = place()
@@ -143,9 +158,12 @@
     cn[...] = lax.dot_general(
         ones, both * both, (((1,), (1,)), ((), ())), precision=HI, preferred_element_type=jnp.float32
     )
+    ch[0], ch[1] = halves(both)
     arrive(swap_w)
+    wh[0], wh[1] = halves(ww[...].reshape(2 * m, -1))
 
     cp = {}
+    kernels = []
 
     def send_parts(g):
         for q in plane_far_first:
@@ -164,17 +182,15 @@
             send_parts(0)
         points = xa[:, rows, :].reshape(PLANE * GROUP, features)
         norms = jnp.sum(points * points, axis=1, keepdims=True)
-        cross = lax.dot_general(
-            points, cc[...].reshape(2 * m, features), (((1,), (1,)), ((), ())),
-            precision=HI, preferred_element_type=jnp.float32,
-        )
+        cross = product(halves(points), (ch[0], ch[1]), ((1,), (1,)), True)
         kernel = jnp.exp(-(norms + cn[0:1, :] - 2.0 * cross) / features)
-        kk[:, rows, :] = kernel.reshape(PLANE, GROUP, 2 * m)
-        part = jnp.dot(
-            kernel, ww[...].reshape(2 * m, -1), precision=HI, preferred_element_type=jnp.float32
-        )
+        kernel_halves = halves(kernel)
+        part = product(kernel_halves, (wh[0], wh[1]), ((1,), (0,)), False)
         pp[:, rows, :] = part.reshape(PLANE, GROUP, -1)
+        kernels.append(kernel)
     send_parts(1)
+    for g in range(2):
+        kt[g, 0], kt[g, 1] = halves(kernels[g].T)
 
     cz = {}
     for g in range(2):
@@ -235,10 +251,8 @@
         rows = slice(g * GROUP, (g + 1) * GROUP)
         for q in range(1, PLANE):
             arrive(dp[g, opposite(q)])
-        term = lax.dot_general(
-            kk[:, rows, :].reshape(PLANE * GROUP, 2 * m),
-            rb[:, rows, :].reshape(PLANE * GROUP, -1),
-            (((0,), (0,)), ((), ())), precision=HI, preferred_element_type=jnp.float32,
+        term = product(
+            (kt[g, 0], kt[g, 1]), halves(rb[:, rows, :].reshape(PLANE * GROUP, -1)), ((1,), (0,)), False
         )
         change = term if change is None else change + term
     uu[...] = change
@@ -257,7 +271,7 @@
     devices = lax.axis_size("wide") * lax.axis_size("narrow")
     all_rows = batch.shape[0] * lax.axis_size("wide")
     pred_scale = 8.0 / math.sqrt(m * devices)
-    f32 = jnp.float32
+    f32, bf16 = jnp.float32, jnp.bfloat16
     vmem = pltpu.VMEM
     dma = pltpu.SemaphoreType.DMA
     xk, rk = features // 128, outputs // 128
@@ -266,10 +280,12 @@
         vmem(targets.shape, f32),
         vmem((2, m, features), f32),
         vmem((2, m, outputs), f32),
+        vmem((2, 2 * m, features), bf16),
+        vmem((2, 2 * m, outputs), bf16),
         vmem((DEPTH, xk, 128), f32),
         vmem((PLANE, DEPTH, features), f32),
         vmem((8, 2 * m), f32),
-        vmem((PLANE, DEPTH, 2 * m), f32),
+        vmem((2, 2, 2 * m, PLANE * GROUP), bf16),
         vmem((PLANE, DEPTH, outputs), f32),
         vmem((PLANE, DEPTH, outputs), f32),
         vmem((DEPTH, rk, 128), f32),
@@ -297,9 +313,9 @@
         out_specs=(pl.BlockSpec(memory_space=pltpu.VMEM),) * 2,
         scratch_shapes=scratch,
         compiler_params=pltpu.CompilerParams(
-            collective_id=0, has_side_effects=True, vmem_limit_bytes=(64 << 20) - (160 << 10)
+            collective_id=0, has_side_effects=True, vmem_limit_bytes=48 << 20
         ),
-    )(batch, targets, centers, weights)
+    )(*(pltpu.with_memory_space_constraint(a, pltpu.HBM) for a in (batch, targets, centers, weights)))
 
 
 def solution(mesh):

time: 67.9 us -> 63.8 us (0.940)
  Pallas kernels: 64.1 us -> 61.7 us
  local copies, waits for them, and re-layouts: 2.92 us -> 1.28 us
    pallas_call x1, Pallas kernels: 64.1 us -> 61.7 us  [shards(): pl.pallas_call(functools.partial(body, pred_scale, 32.0 / all_rows), out_...]
    unnamed x4 -> x2, local copies, waits for them, and re-layouts: 2.92 us -> 1.28 us
where the time goes in v4:
time: 63.8 us; the launch traced here: 63.6 us
  Pallas kernels  61.7 us (97%)
  local copies, waits for them, and re-layouts  1.28 us (2%)
  between operations  0.64 us (1%)
    pallas_call x1, Pallas kernels, shards(): pl.pallas_call(functools.partial(body, pred_scale, 32.0 / all_rows), out_...  61.7 us
    unnamed x2, local copies, waits for them, and re-layouts  1.28 us

profile of v4, /device:TPU:1, one launch (start us, length us, event | category | flops | bytes accessed | tf_op | source)
XLA Modules:
  0.0 63.6 jit_solution(9852320756024196097)
XLA Ops:
  0.6 61.7 %shard_map.59 = (f32[1,512]{1,0:T(1,128)S(1)}, f32[128,512]{1,0:T(8,128)S(1)}) custom-call(f32[16,768]{1,0:T(8,128)} %batch_ref.1, f32[1,512]{1,0:T(1,128)} %targets_ref.1, f32[128,768]{1,0:T(8,128)} %centers_ref.1, f32[128,512]{1,0:T(8,128)} %weights_ref.1), custom_call_target="tpu_custom_call" | custom-call | tf_op jit(solution)/shard_map/pallas_call | solution.py:306
  62.3 0.6 copy.8
  62.9 0.7 %copy.9 = f32[128,512]{1,0:T(8,128)} copy(f32[128,512]{1,0:T(8,128)S(1)} %get-tuple-element.5) | data formatting | bytes 524288

commit v5 on v4

--- a/solution.py
+++ b/solution.py
@@ -12,6 +12,8 @@
 PLANE = SIDE * SIDE
 GROUP = 8
 REACH = 4
+SPREAD = (0, 1, -1, 2)
+PIECES = ((0, 1), (1, 2), (3, 1))
 NEAR = 4
 MESH = pl.DeviceIdType.MESH
 HI = lax.Precision.HIGHEST
@@ -50,15 +52,15 @@
 
 def body(
     pred_scale, step, batch_ref, targets_ref, centers_ref, weights_ref, res_ref, new_ref,
-    xb, tg, cc, ww, ch, wh, z1, xa, cn, kt, pp, cb, s3, zb, rz, rb, uu, ub,
-    lsem, core_s, core_r, az_s, az_r, ap_s, ap_r, cp_s, cp_r, cz_s, cz_r, dz_s, dz_r, dp_s, dp_r,
+    xb, tg, cc, ww, ch, wh, z1, xa, cn, kt, pp, cb, s3, t4, s4, nb, ft, fb, rb, uu, ub,
+    lsem, core_s, core_r, az_s, az_r, ap_s, ap_r, cp_s, cp_r, nz_s, nz_r, fz_s, fz_r, gz_s, gz_r, dp_s, dp_r,
 ):
     x, y, z, core, n = place()
     features = cc.shape[2]
     m = cc.shape[1]
     lanes = 128
     xk = features // lanes
-    rk = rb.shape[2] // lanes
+    rk = rb.shape[2]
 
     loads = [
         pltpu.make_async_copy(batch_ref, xb, lsem.at[0]),
@@ -148,9 +150,6 @@
             )
             go(ap[g, q])
 
-    def landed_z(copies, s):
-        arrive(copies[(NEAR - s) % DEPTH])
-
     got(loads[1])
     arrive(swap_c)
     both = cc[...].reshape(2 * m, features)
@@ -187,12 +186,29 @@
         kernel_halves = halves(kernel)
         part = product(kernel_halves, (wh[0], wh[1]), ((1,), (0,)), False)
         pp[:, rows, :] = part.reshape(PLANE, GROUP, -1)
-        kernels.append(kernel)
+        kernels.append(kernel_halves)
     send_parts(1)
-    for g in range(2):
-        kt[g, 0], kt[g, 1] = halves(kernels[g].T)
-
-    cz = {}
+
+    wide_shape = (PLANE * GROUP, PLANE * DEPTH)
+    row, col = (lax.broadcasted_iota(jnp.int32, wide_shape, axis) for axis in (0, 1))
+    block, step4 = col // (PLANE * 4), col % 4
+    shift = jnp.zeros_like(col)
+    for b in range(1, 4):
+        shift = jnp.where(block == b, SPREAD[b], shift)
+    wanted = (4 * step4 - shift + DEPTH) % DEPTH
+    same_plane = row // GROUP == col % (PLANE * 4) // 4
+    for half in range(2):
+        turned = None
+        for g in range(2):
+            pick = jnp.where(same_plane & (wanted == row % GROUP + g * GROUP), 1.0, 0.0).astype(jnp.bfloat16)
+            term = lax.dot_general(
+                kernels[g][half], pick, (((0,), (0,)), ((), ())), preferred_element_type=jnp.float32
+            )
+            turned = term if turned is None else turned + term
+        kt[half] = turned.astype(jnp.bfloat16)
+
+    for k in range(rk):
+        t4[k : k + 1, :] = tg[:, k * lanes : (k + 1) * lanes]
     for g in range(2):
         rows = slice(g * GROUP, (g + 1) * GROUP)
         for q in range(1, PLANE):
@@ -202,58 +218,59 @@
             total = total + cb[q, rows, :]
         for k in range(rk):
             s3[rows, k, :] = total[:, k * lanes : (k + 1) * lanes]
-        for d in far_first:
-            s = (NEAR + d) % DEPTH
-            if s // GROUP == g:
-                cz[d] = remote(
-                    s3.at[s], zb.at[(NEAR - d) % DEPTH], cz_s.at[d], cz_r.at[(NEAR - d) % DEPTH], z_peers[d]
-                )
-                go(cz[d])
-
-    own = s3[NEAR]
-    for s in range(DEPTH):
-        if s != NEAR:
-            landed_z(cz, s)
-            own = own + zb[s]
-    own = own * pred_scale
-    for k in range(rk):
-        piece = own[k : k + 1, :] - tg[:, k * lanes : (k + 1) * lanes]
-        rz[NEAR, k : k + 1, :] = piece
-        res_ref[:, k * lanes : (k + 1) * lanes] = piece
-
-    dz = {
-        d: remote(
-            rz.at[NEAR], rz.at[(NEAR - d) % DEPTH], dz_s.at[d], dz_r.at[(NEAR - d) % DEPTH], z_peers[d]
+        for s in range(g * GROUP, (g + 1) * GROUP):
+            scaled = s3[s] * pred_scale
+            s4[s % 4, s // 4] = scaled - t4[...] if s == NEAR else scaled
+
+    nz = {}
+    for j, e in ((2, -2), (0, 1), (1, -1)):
+        nz[j] = remote(s4.at[e % 4], nb.at[j], nz_s.at[j], nz_r.at[j], z_peers[e % DEPTH])
+        go(nz[j])
+    for j in (0, 1, 2):
+        arrive(nz[j])
+    for i in range(4):
+        ft[i] = s4[0, i] + nb[0, i] + nb[1, (i - 1) % 4] + nb[2, (i - 1) % 4]
+    fz = {}
+    for j in (2, 1, 3):
+        fz[j] = remote(ft, fb.at[j], fz_s.at[j], fz_r.at[j], z_peers[DEPTH - 4 * j])
+        go(fz[j])
+    for j in (1, 3, 2):
+        arrive(fz[j])
+    for i in range(4):
+        rb[0, i] = ft[i] + fb[1, (i - 1) % 4] + fb[2, (i - 2) % 4] + fb[3, (i - 3) % 4]
+
+    gz = {}
+    for b in (3, 1, 2):
+        gz[b] = remote(
+            rb.at[0, pl.ds(0, 4)], rb.at[b, pl.ds(0, 4)], gz_s.at[b], gz_r.at[b], z_peers[SPREAD[b] % DEPTH]
         )
-        for d in range(1, DEPTH)
-    }
-    for d in far_first:
-        go(dz[d])
-
+        go(gz[b])
     dp = {}
-    for g in range(2):
-        rows = slice(g * GROUP, (g + 1) * GROUP)
-        for s in range(g * GROUP, (g + 1) * GROUP):
-            if s != NEAR:
-                landed_z(dz, s)
-        for k in range(rk):
-            rb[0, rows, k * lanes : (k + 1) * lanes] = rz[rows, k, :]
+    for p, (first, count) in enumerate(PIECES):
+        for b in range(first, first + count):
+            if b:
+                arrive(gz[b])
         for q in plane_far_first:
-            dp[g, q] = remote(
-                rb.at[0, pl.ds(g * GROUP, GROUP)],
-                rb.at[opposite(q), pl.ds(g * GROUP, GROUP)],
-                dp_s.at[g, q], dp_r.at[g, opposite(q)], p_peers[q],
+            dp[p, q] = remote(
+                rb.at[pl.ds(first, count), pl.ds(0, 4)],
+                rb.at[pl.ds(first, count), pl.ds(opposite(q) * 4, 4)],
+                dp_s.at[p, q], dp_r.at[p, opposite(q)], p_peers[q],
             )
-            go(dp[g, q])
+            go(dp[p, q])
+        if p == 0:
+            for k in range(rk):
+                res_ref[:, k * lanes : (k + 1) * lanes] = rb[0, 1, k : k + 1, :]
 
     change = None
-    for g in range(2):
-        rows = slice(g * GROUP, (g + 1) * GROUP)
-        for q in range(1, PLANE):
-            arrive(dp[g, opposite(q)])
-        term = product(
-            (kt[g, 0], kt[g, 1]), halves(rb[:, rows, :].reshape(PLANE * GROUP, -1)), ((1,), (0,)), False
+    for h in range(2):
+        for p in ((0, 1), (2,))[h]:
+            for q in range(1, PLANE):
+                arrive(dp[p, opposite(q)])
+        rows = jnp.concatenate(
+            [rb[2 * h : 2 * h + 2, :, k, :].reshape(PLANE * GROUP, lanes) for k in range(rk)], axis=1
         )
+        columns = slice(h * PLANE * GROUP, (h + 1) * PLANE * GROUP)
+        term = product((kt[0, :, columns], kt[1, :, columns]), halves(rows), ((1,), (0,)), False)
         change = term if change is None else change + term
     uu[...] = change
     swap_u = remote(uu.at[pl.ds(m, m)], ub, core_s.at[2], core_r.at[2], mate)
@@ -285,13 +302,16 @@
         vmem((DEPTH, xk, 128), f32),
         vmem((PLANE, DEPTH, features), f32),
         vmem((8, 2 * m), f32),
-        vmem((2, 2, 2 * m, PLANE * GROUP), bf16),
+        vmem((2, 2 * m, PLANE * DEPTH), bf16),
         vmem((PLANE, DEPTH, outputs), f32),
         vmem((PLANE, DEPTH, outputs), f32),
         vmem((DEPTH, rk, 128), f32),
-        vmem((DEPTH, rk, 128), f32),
-        vmem((DEPTH, rk, 128), f32),
-        vmem((PLANE, DEPTH, outputs), f32),
+        vmem((rk, 128), f32),
+        vmem((4, 4, rk, 128), f32),
+        vmem((3, 4, rk, 128), f32),
+        vmem((4, rk, 128), f32),
+        vmem((4, 4, rk, 128), f32),
+        vmem((4, PLANE * 4, rk, 128), f32),
         vmem((2 * m, outputs), f32),
         vmem((m, outputs), f32),
         dma((4,)),
@@ -299,9 +319,10 @@
         dma((DEPTH,)), dma((DEPTH,)),
         dma((2, PLANE)), dma((2, PLANE)),
         dma((2, PLANE)), dma((2, PLANE)),
-        dma((DEPTH,)), dma((DEPTH,)),
-        dma((DEPTH,)), dma((DEPTH,)),
-        dma((2, PLANE)), dma((2, PLANE)),
+        dma((3,)), dma((3,)),
+        dma((4,)), dma((4,)),
+        dma((4,)), dma((4,)),
+        dma((len(PIECES), PLANE)), dma((len(PIECES), PLANE)),
     ]
     return pl.pallas_call(
         functools.partial(body, pred_scale, 32.0 / all_rows),

time: 63.8 us -> 64.8 us (1.016)
  Pallas kernels: 61.7 us -> 62.7 us
    pallas_call x1, Pallas kernels: 61.7 us -> 62.7 us  [shards(): pl.pallas_call(functools.partial(body, pred_scale, 32.0 / all_rows), out_...]
where the time goes in v5:
time: 64.8 us; the launch traced here: 64.7 us
  Pallas kernels  62.7 us (97%)
  local copies, waits for them, and re-layouts  1.28 us (2%)
    pallas_call x1, Pallas kernels, shards(): pl.pallas_call(functools.partial(body, pred_scale, 32.0 / all_rows), out_...  62.7 us

profile of v5, /device:TPU:1, one launch (start us, length us, event | category | flops | bytes accessed | tf_op | source)
XLA Modules:
  0.0 64.7 jit_solution(9875154945677606827)
XLA Ops:
  0.6 62.7 %shard_map.59 = (f32[1,512]{1,0:T(1,128)S(1)}, f32[128,512]{1,0:T(8,128)S(1)}) custom-call(f32[16,768]{1,0:T(8,128)} %batch_ref.1, f32[1,512]{1,0:T(1,128)} %targets_ref.1, f32[128,768]{1,0:T(8,128)} %centers_ref.1, f32[128,512]{1,0:T(8,128)} %weights_ref.1), custom_call_target="tpu_custom_call" | custom-call | tf_op jit(solution)/shard_map/pallas_call | solution.py:327
  63.4 0.6 copy.8
  64.0 0.7 %copy.9 = f32[128,512]{1,0:T(8,128)} copy(f32[128,512]{1,0:T(8,128)S(1)} %get-tuple-element.5) | data formatting | bytes 524288

commit v6 on v4

--- a/solution.py
+++ b/solution.py
@@ -69,11 +69,18 @@
     for load in loads:
         load.start()
 
-    mate = name_of(x, y, z, 1 - core)
-    z_peers = {d: name_of(x, y, lax.rem(z + d, DEPTH), core) for d in range(1, DEPTH)}
+    def around(at, size):
+        return [at] + [jnp.where(at + d >= size, at + d - size, at + d) for d in range(1, size)]
+
+    zs, xs, ys = around(z, DEPTH), around(x, SIDE), around(y, SIDE)
+    here = lax.axis_index("wide") - z
+    x_low = [lax.rem(v, 2) * DEPTH + z for v in xs]
+    x_high = [lax.div(v, 2) * CORES + core for v in xs]
+    y_high = [v * (2 * CORES) for v in ys]
+    mate = (here + z, n + 1 - 2 * core)
+    z_peers = {d: (here + zs[d], n) for d in range(1, DEPTH)}
     p_peers = {
-        q: name_of(lax.rem(x + q // SIDE, SIDE), lax.rem(y + q % SIDE, SIDE), z, core)
-        for q in range(1, PLANE)
+        q: (x_low[q // SIDE], x_high[q // SIDE] + y_high[q % SIDE]) for q in range(1, PLANE)
     }
     greeted = [mate, *p_peers.values()]
     greeted += [z_peers[d % DEPTH] for d in range(-REACH, REACH + 1) if d]
@@ -87,17 +94,11 @@
             device_id=peer, device_id_type=MESH,
         )
 
-    sent = []
-
-    def go(copy):
-        copy.start()
-        sent.append(copy)
-
-    def arrive(copy):
-        copy.wait_recv()
-
-    def got(copy):
-        copy.wait()
+    def all_in(buffer, sem):
+        remote(buffer, buffer, sem, sem, mate).wait_recv()
+
+    def all_out(buffer, sem):
+        remote(buffer, buffer, sem, sem, mate).wait_send()
 
     def opposite(q):
         return (-(q // SIDE)) % SIDE * SIDE + (-(q % SIDE)) % SIDE
@@ -105,79 +106,63 @@
     far_first = sorted(range(1, DEPTH), key=lambda d: -min(d, DEPTH - d))
     plane_far_first = sorted(range(1, PLANE), key=lambda q: -hops(q // SIDE) - hops(q % SIDE))
 
-    got(loads[0])
+    loads[0].wait()
     mine = xb[pl.ds(n, 1), :]
     for k in range(xk):
         z1[NEAR, k : k + 1, :] = mine[:, k * lanes : (k + 1) * lanes]
     pl.semaphore_wait(barrier, len(greeted))
 
-    az = {}
-
-    def along_z(source, d, slot):
-        az[slot] = remote(z1.at[source], z1.at[slot], az_s.at[slot], az_r.at[slot], z_peers[d % DEPTH])
-        go(az[slot])
+    def along_z(first, count, d, there, part):
+        remote(
+            z1.at[pl.ds(first, count)], z1.at[pl.ds(there, count)], az_s.at[0], az_r.at[part], z_peers[d % DEPTH]
+        ).start()
 
     for d in (4, -4, 3, -3, 2, -2, 1, -1):
-        along_z(NEAR, d, NEAR - d)
-    got(loads[2])
+        slot = NEAR - d
+        along_z(NEAR, 1, d, slot, 0 if slot < NEAR else 1 if slot < GROUP else 2)
+    loads[2].wait()
     swap_c = remote(cc.at[0], cc.at[1], core_s.at[0], core_r.at[0], mate)
-    go(swap_c)
-    got(loads[3])
+    swap_c.start()
+    loads[3].wait()
     swap_w = remote(ww.at[0], ww.at[1], core_s.at[1], core_r.at[1], mate)
-    go(swap_w)
-    for s in (3, 5, 2, 6, 1, 7, 0):
-        arrive(az[s])
-        if s < NEAR:
-            along_z(s, REACH, s + 12)
-        else:
-            along_z(s, -REACH, s + 4)
-
-    ap = {}
-    for g in range(2):
-        rows = slice(g * GROUP, (g + 1) * GROUP)
+    swap_w.start()
+    all_in(z1.at[pl.ds(0, 4)], az_r.at[0])
+    along_z(0, 4, REACH, 12, 2)
+    all_in(z1.at[pl.ds(5, 3)], az_r.at[1])
+    along_z(5, 3, -REACH, 9, 2)
+
+    for g in range(2):
+        rows = slice(g * GROUP, (g + 1) * GROUP)
+        here = pl.ds(g * GROUP, GROUP)
         if g == 1:
-            for s in range(GROUP, DEPTH):
-                arrive(az[s])
+            all_in(z1.at[here], az_r.at[2])
         for k in range(xk):
             xa[0, rows, k * lanes : (k + 1) * lanes] = z1[rows, k, :]
         for q in plane_far_first:
-            ap[g, q] = remote(
-                xa.at[0, pl.ds(g * GROUP, GROUP)],
-                xa.at[opposite(q), pl.ds(g * GROUP, GROUP)],
-                ap_s.at[g, q], ap_r.at[g, opposite(q)], p_peers[q],
-            )
-            go(ap[g, q])
-
-    def landed_z(copies, s):
-        arrive(copies[(NEAR - s) % DEPTH])
-
-    got(loads[1])
-    arrive(swap_c)
+            remote(xa.at[0, here], xa.at[opposite(q), here], ap_s.at[0], ap_r.at[g], p_peers[q]).start()
+
+    loads[1].wait()
+    swap_c.wait_recv()
     both = cc[...].reshape(2 * m, features)
     ones = jnp.ones((8, features), jnp.float32)
     cn[...] = lax.dot_general(
         ones, both * both, (((1,), (1,)), ((), ())), precision=HI, preferred_element_type=jnp.float32
     )
     ch[0], ch[1] = halves(both)
-    arrive(swap_w)
+    swap_w.wait_recv()
     wh[0], wh[1] = halves(ww[...].reshape(2 * m, -1))
 
-    cp = {}
     kernels = []
+    others = pl.ds(1, PLANE - 1)
 
     def send_parts(g):
+        here = pl.ds(g * GROUP, GROUP)
         for q in plane_far_first:
-            cp[g, q] = remote(
-                pp.at[q, pl.ds(g * GROUP, GROUP)],
-                cb.at[opposite(q), pl.ds(g * GROUP, GROUP)],
-                cp_s.at[g, q], cp_r.at[g, opposite(q)], p_peers[q],
-            )
-            go(cp[g, q])
-
-    for g in range(2):
-        rows = slice(g * GROUP, (g + 1) * GROUP)
-        for q in range(1, PLANE):
-            arrive(ap[g, opposite(q)])
+            remote(pp.at[q, here], cb.at[opposite(q), here], cp_s.at[0], cp_r.at[g], p_peers[q]).start()
+
+    for g in range(2):
+        rows = slice(g * GROUP, (g + 1) * GROUP)
+        all_in(xa.at[others, pl.ds(g * GROUP, GROUP)], ap_r.at[g])
         if g == 1:
             send_parts(0)
         points = xa[:, rows, :].reshape(PLANE * GROUP, features)
@@ -192,11 +177,9 @@
     for g in range(2):
         kt[g, 0], kt[g, 1] = halves(kernels[g].T)
 
-    cz = {}
-    for g in range(2):
-        rows = slice(g * GROUP, (g + 1) * GROUP)
-        for q in range(1, PLANE):
-            arrive(cp[g, opposite(q)])
+    for g in range(2):
+        rows = slice(g * GROUP, (g + 1) * GROUP)
+        all_in(cb.at[others, pl.ds(g * GROUP, GROUP)], cp_r.at[g])
         total = pp[0, rows, :]
         for q in range(1, PLANE):
             total = total + cb[q, rows, :]
@@ -205,64 +188,53 @@
         for d in far_first:
             s = (NEAR + d) % DEPTH
             if s // GROUP == g:
-                cz[d] = remote(
-                    s3.at[s], zb.at[(NEAR - d) % DEPTH], cz_s.at[d], cz_r.at[(NEAR - d) % DEPTH], z_peers[d]
-                )
-                go(cz[d])
+                remote(s3.at[s], zb.at[DEPTH - 1 - d], cz_s.at[0], cz_r.at[0], z_peers[d]).start()
 
     own = s3[NEAR]
-    for s in range(DEPTH):
-        if s != NEAR:
-            landed_z(cz, s)
-            own = own + zb[s]
+    all_in(zb, cz_r.at[0])
+    for s in range(DEPTH - 1):
+        own = own + zb[s]
     own = own * pred_scale
     for k in range(rk):
         piece = own[k : k + 1, :] - tg[:, k * lanes : (k + 1) * lanes]
         rz[NEAR, k : k + 1, :] = piece
         res_ref[:, k * lanes : (k + 1) * lanes] = piece
 
-    dz = {
-        d: remote(
-            rz.at[NEAR], rz.at[(NEAR - d) % DEPTH], dz_s.at[d], dz_r.at[(NEAR - d) % DEPTH], z_peers[d]
-        )
-        for d in range(1, DEPTH)
-    }
     for d in far_first:
-        go(dz[d])
-
-    dp = {}
-    for g in range(2):
-        rows = slice(g * GROUP, (g + 1) * GROUP)
-        for s in range(g * GROUP, (g + 1) * GROUP):
-            if s != NEAR:
-                landed_z(dz, s)
+        slot = (NEAR - d) % DEPTH
+        remote(rz.at[NEAR], rz.at[slot], dz_s.at[0], dz_r.at[slot // GROUP], z_peers[d]).start()
+
+    for g in range(2):
+        rows = slice(g * GROUP, (g + 1) * GROUP)
+        here = pl.ds(g * GROUP, GROUP)
+        all_in(rz.at[pl.ds(g * GROUP, GROUP - 1 + g)], dz_r.at[g])
         for k in range(rk):
             rb[0, rows, k * lanes : (k + 1) * lanes] = rz[rows, k, :]
         for q in plane_far_first:
-            dp[g, q] = remote(
-                rb.at[0, pl.ds(g * GROUP, GROUP)],
-                rb.at[opposite(q), pl.ds(g * GROUP, GROUP)],
-                dp_s.at[g, q], dp_r.at[g, opposite(q)], p_peers[q],
-            )
-            go(dp[g, q])
+            remote(rb.at[0, here], rb.at[opposite(q), here], dp_s.at[0], dp_r.at[g], p_peers[q]).start()
 
     change = None
     for g in range(2):
         rows = slice(g * GROUP, (g + 1) * GROUP)
-        for q in range(1, PLANE):
-            arrive(dp[g, opposite(q)])
+        all_in(rb.at[others, pl.ds(g * GROUP, GROUP)], dp_r.at[g])
         term = product(
             (kt[g, 0], kt[g, 1]), halves(rb[:, rows, :].reshape(PLANE * GROUP, -1)), ((1,), (0,)), False
         )
         change = term if change is None else change + term
     uu[...] = change
     swap_u = remote(uu.at[pl.ds(m, m)], ub, core_s.at[2], core_r.at[2], mate)
-    go(swap_u)
-    arrive(swap_u)
+    swap_u.start()
+    swap_u.wait_recv()
     new_ref[...] = ww[0] - step * (uu[0:m, :] + ub[...])
 
-    for copy in sent:
-        copy.wait_send()
+    for swap in (swap_c, swap_w, swap_u):
+        swap.wait_send()
+    all_out(z1.at[pl.ds(0, DEPTH - 1)], az_s.at[0])
+    all_out(xa.at[others], ap_s.at[0])
+    all_out(pp.at[others], cp_s.at[0])
+    all_out(zb, cz_s.at[0])
+    all_out(rz.at[pl.ds(0, DEPTH - 1)], dz_s.at[0])
+    all_out(rb.at[others], dp_s.at[0])
 
 
 def shards(batch, targets, centers, weights):
@@ -289,19 +261,19 @@
         vmem((PLANE, DEPTH, outputs), f32),
         vmem((PLANE, DEPTH, outputs), f32),
         vmem((DEPTH, rk, 128), f32),
-        vmem((DEPTH, rk, 128), f32),
+        vmem((DEPTH - 1, rk, 128), f32),
         vmem((DEPTH, rk, 128), f32),
         vmem((PLANE, DEPTH, outputs), f32),
         vmem((2 * m, outputs), f32),
         vmem((m, outputs), f32),
         dma((4,)),
         dma((3,)), dma((3,)),
-        dma((DEPTH,)), dma((DEPTH,)),
-        dma((2, PLANE)), dma((2, PLANE)),
-        dma((2, PLANE)), dma((2, PLANE)),
-        dma((DEPTH,)), dma((DEPTH,)),
-        dma((DEPTH,)), dma((DEPTH,)),
-        dma((2, PLANE)), dma((2, PLANE)),
+        dma((1,)), dma((3,)),
+        dma((1,)), dma((2,)),
+        dma((1,)), dma((2,)),
+        dma((1,)), dma((1,)),
+        dma((1,)), dma((2,)),
+        dma((1,)), dma((2,)),
     ]
     return pl.pallas_call(
         functools.partial(body, pred_scale, 32.0 / all_rows),

time: 63.8 us -> 61 us (0.956)
  Pallas kernels: 61.7 us -> 59 us
    pallas_call x1, Pallas kernels: 61.7 us -> 59 us  [shards(): pl.pallas_call(functools.partial(body, pred_scale, 32.0 / all_rows), out_...]
where the time goes in v6:
time: 61 us; the launch traced here: 60.9 us
  Pallas kernels  59 us (97%)
  local copies, waits for them, and re-layouts  1.28 us (2%)
  between operations  0.64 us (1%)
    pallas_call x1, Pallas kernels, shards(): pl.pallas_call(functools.partial(body, pred_scale, 32.0 / all_rows), out_...  59 us
    unnamed x2, local copies, waits for them, and re-layouts  1.28 us

profile of v6, /device:TPU:1, one launch (start us, length us, event | category | flops | bytes accessed | tf_op | source)
XLA Modules:
  0.0 60.9 jit_solution(1910367002309434693)
XLA Ops:
  0.6 59.0 %shard_map.59 = (f32[1,512]{1,0:T(1,128)S(1)}, f32[128,512]{1,0:T(8,128)S(1)}) custom-call(f32[16,768]{1,0:T(8,128)} %batch_ref.1, f32[1,512]{1,0:T(1,128)} %targets_ref.1, f32[128,768]{1,0:T(8,128)} %centers_ref.1, f32[128,512]{1,0:T(8,128)} %weights_ref.1), custom_call_target="tpu_custom_call" | custom-call | tf_op jit(solution)/shard_map/pallas_call | solution.py:278
  59.6 0.6 copy.8
  60.2 0.7 %copy.9 = f32[128,512]{1,0:T(8,128)} copy(f32[128,512]{1,0:T(8,128)S(1)} %get-tuple-element.5) | data formatting | bytes 524288

commit v7 on v6

--- a/solution.py
+++ b/solution.py
@@ -213,21 +213,31 @@
         for q in plane_far_first:
             remote(rb.at[0, here], rb.at[opposite(q), here], dp_s.at[0], dp_r.at[g], p_peers[q]).start()
 
-    change = None
-    for g in range(2):
-        rows = slice(g * GROUP, (g + 1) * GROUP)
+    def update_part(g, residual, lo, cols):
+        return product(
+            (kt[g, 0, lo : lo + m, :], kt[g, 1, lo : lo + m, :]),
+            tuple(half[:, cols] for half in residual), ((1,), (0,)), False,
+        )
+
+    parts = [slice(c * (rk * lanes // 2), (c + 1) * (rk * lanes // 2)) for c in range(2)]
+    for g in range(2):
         all_in(rb.at[others, pl.ds(g * GROUP, GROUP)], dp_r.at[g])
-        term = product(
-            (kt[g, 0], kt[g, 1]), halves(rb[:, rows, :].reshape(PLANE * GROUP, -1)), ((1,), (0,)), False
-        )
-        change = term if change is None else change + term
-    uu[...] = change
-    swap_u = remote(uu.at[pl.ds(m, m)], ub, core_s.at[2], core_r.at[2], mate)
-    swap_u.start()
-    swap_u.wait_recv()
-    new_ref[...] = ww[0] - step * (uu[0:m, :] + ub[...])
-
-    for swap in (swap_c, swap_w, swap_u):
+        residual = halves(rb[:, g * GROUP : (g + 1) * GROUP, :].reshape(PLANE * GROUP, -1))
+        if g == 0:
+            for c in range(2):
+                uu[c] = update_part(g, residual, m, parts[c])
+            new_ref[...] = ww[0] - step * update_part(g, residual, 0, slice(None))
+    swap_u = []
+    for c in range(2):
+        uu[c] = uu[c] + update_part(1, residual, m, parts[c])
+        swap_u.append(remote(uu.at[c], ub.at[c], core_s.at[2 + c], core_r.at[2 + c], mate))
+        swap_u[c].start()
+    for c in range(2):
+        own_part = new_ref[:, parts[c]] - step * update_part(1, residual, 0, parts[c])
+        swap_u[c].wait_recv()
+        new_ref[:, parts[c]] = own_part - step * ub[c]
+
+    for swap in (swap_c, swap_w, *swap_u):
         swap.wait_send()
     all_out(z1.at[pl.ds(0, DEPTH - 1)], az_s.at[0])
     all_out(xa.at[others], ap_s.at[0])
@@ -235,6 +245,17 @@
     all_out(zb, cz_s.at[0])
     all_out(rz.at[pl.ds(0, DEPTH - 1)], dz_s.at[0])
     all_out(rb.at[others], dp_s.at[0])
+
+
+def place_outputs(res_ref, new_ref, res_out, new_out, sems):
+    copies = [
+        pltpu.make_async_copy(new_ref, new_out, sems.at[0]),
+        pltpu.make_async_copy(res_ref, res_out, sems.at[1]),
+    ]
+    for copy in copies:
+        copy.start()
+    for copy in copies:
+        copy.wait()
 
 
 def shards(batch, targets, centers, weights):
@@ -264,10 +285,10 @@
         vmem((DEPTH - 1, rk, 128), f32),
         vmem((DEPTH, rk, 128), f32),
         vmem((PLANE, DEPTH, outputs), f32),
-        vmem((2 * m, outputs), f32),
-        vmem((m, outputs), f32),
+        vmem((2, m, outputs // 2), f32),
+        vmem((2, m, outputs // 2), f32),
         dma((4,)),
-        dma((3,)), dma((3,)),
+        dma((4,)), dma((4,)),
         dma((1,)), dma((3,)),
         dma((1,)), dma((2,)),
         dma((1,)), dma((2,)),
@@ -275,7 +296,7 @@
         dma((1,)), dma((2,)),
         dma((1,)), dma((2,)),
     ]
-    return pl.pallas_call(
+    outputs_made = pl.pallas_call(
         functools.partial(body, pred_scale, 32.0 / all_rows),
         out_shape=(
             jax.ShapeDtypeStruct(targets.shape, f32),
@@ -288,6 +309,17 @@
             collective_id=0, has_side_effects=True, vmem_limit_bytes=48 << 20
         ),
     )(*(pltpu.with_memory_space_constraint(a, pltpu.HBM) for a in (batch, targets, centers, weights)))
+    return pl.pallas_call(
+        place_outputs,
+        out_shape=(
+            jax.ShapeDtypeStruct(targets.shape, f32),
+            jax.ShapeDtypeStruct(weights.shape, f32),
+        ),
+        in_specs=[pl.BlockSpec(memory_space=pltpu.VMEM)] * 2,
+        out_specs=(pl.BlockSpec(memory_space=pltpu.HBM),) * 2,
+        scratch_shapes=[dma((2,))],
+        compiler_params=pltpu.CompilerParams(vmem_limit_bytes=8 << 20),
+    )(*outputs_made)
 
 
 def solution(mesh):

time: 61 us -> 60.2 us (0.987)
  local copies, waits for them, and re-layouts: 1.28 us -> 0 us
    unnamed x2 -> x0, local copies, waits for them, and re-layouts: 1.28 us -> none
    pallas_call x0 -> x1, Pallas kernels: none -> 0.72 us  [shards(): pl.pallas_call(place_outputs, out_shape=(jax.ShapeDtypeStruct(targets.sha...]
where the time goes in v7:
time: 60.2 us; the launch traced here: 60.1 us
  Pallas kernels  59.4 us (99%)
  between operations  0.64 us (1%)
    pallas_call x1, Pallas kernels, shards(): pl.pallas_call(functools.partial(body, pred_scale, 32.0 / all_rows), out_...  58.7 us

profile of v7, /device:TPU:1, one launch (start us, length us, event | category | flops | bytes accessed | tf_op | source)
XLA Modules:
  0.0 60.1 jit_solution(6178758770075301474)
XLA Ops:
  0.6 58.7 %shard_map.59 = (f32[1,512]{1,0:T(1,128)S(1)}, f32[128,512]{1,0:T(8,128)S(1)}) custom-call(f32[16,768]{1,0:T(8,128)} %batch_ref.1, f32[1,512]{1,0:T(1,128)} %targets_ref.1, f32[128,768]{1,0:T(8,128)} %centers_ref.1, f32[128,512]{1,0:T(8,128)} %weights_ref.1), custom_call_target="tpu_custom_call" | custom-call | tf_op jit(solution)/shard_map/pallas_call | solution.py:299
  59.3 0.7 %shard_map.60 = (f32[1,512]{1,0:T(1,128)}, f32[128,512]{1,0:T(8,128)}) custom-call(f32[1,512]{1,0:T(1,128)S(1)} %get-tuple-element.4.res_ref, f32[128,512]{1,0:T(8,128)S(1)} %get-tuple-element.5.new_ref), custom_call_target="tpu_custom_call" | custom-call | tf_op jit(solution)/shard_map/pallas_call | solution.py:312

commit v8 on v7

--- a/solution.py
+++ b/solution.py
@@ -66,8 +66,7 @@
         pltpu.make_async_copy(centers_ref, cc.at[0], lsem.at[2]),
         pltpu.make_async_copy(weights_ref, ww.at[0], lsem.at[3]),
     ]
-    for load in loads:
-        load.start()
+    loads[0].start()
 
     def around(at, size):
         return [at] + [jnp.where(at + d >= size, at + d - size, at + d) for d in range(1, size)]
@@ -82,11 +81,14 @@
     p_peers = {
         q: (x_low[q // SIDE], x_high[q // SIDE] + y_high[q % SIDE]) for q in range(1, PLANE)
     }
-    greeted = [mate, *p_peers.values()]
-    greeted += [z_peers[d % DEPTH] for d in range(-REACH, REACH + 1) if d]
+    greeted = [z_peers[d % DEPTH] for d in (4, -4, 3, -3, 2, -2, 1, -1)]
+    greeted += [p_peers[q] for q in sorted(p_peers, key=lambda q: -hops(q // SIDE) - hops(q % SIDE))]
+    greeted.append(mate)
     barrier = pltpu.get_barrier_semaphore()
     for peer in greeted:
         pl.semaphore_signal(barrier, inc=1, device_id=peer, device_id_type=MESH)
+    for load in loads[1:]:
+        load.start()
 
     def remote(src, dst, send, recv, peer):
         return pltpu.make_async_remote_copy(

time: 60.2 us -> 59.9 us (level)
  no operation moved by 1% of the time
where the time goes in v8:
time: 59.9 us; the launch traced here: 59.8 us
  Pallas kernels  59.1 us (99%)
  between operations  0.64 us (1%)
    pallas_call x1, Pallas kernels, shards(): pl.pallas_call(functools.partial(body, pred_scale, 32.0 / all_rows), out_...  58.4 us

profile of v8, /device:TPU:1, one launch (start us, length us, event | category | flops | bytes accessed | tf_op | source)
XLA Modules:
  0.0 59.8 jit_solution(6953082581269487468)
XLA Ops:
  0.6 58.4 %shard_map.59 = (f32[1,512]{1,0:T(1,128)S(1)}, f32[128,512]{1,0:T(8,128)S(1)}) custom-call(f32[16,768]{1,0:T(8,128)} %batch_ref.1, f32[1,512]{1,0:T(1,128)} %targets_ref.1, f32[128,768]{1,0:T(8,128)} %centers_ref.1, f32[128,512]{1,0:T(8,128)} %weights_ref.1), custom_call_target="tpu_custom_call" | custom-call | tf_op jit(solution)/shard_map/pallas_call | solution.py:301
  59.1 0.7 %shard_map.60 = (f32[1,512]{1,0:T(1,128)}, f32[128,512]{1,0:T(8,128)}) custom-call(f32[1,512]{1,0:T(1,128)S(1)} %get-tuple-element.4.res_ref, f32[128,512]{1,0:T(8,128)S(1)} %get-tuple-element.5.new_ref), custom_call_target="tpu_custom_call" | custom-call | tf_op jit(solution)/shard_map/pallas_call | solution.py:314
